TPU v7x, 128 devices: a whole 4x4x4 slice. The times are simulated.
128 devices in a mesh: bin: 8 (over z_hi, y), row: 4 (over x), col: 4 (over z_lo, core).
Axes of the slice: x: 4, y: 4, z: 4 (z_hi: 2, z_lo: 2; z = z_hi * 2 + z_lo), core: 2. Of those that a mesh axis runs over, the one named last changes fastest.
Arguments:
- snapshots: bfloat16 [4096, 64, 64], P('row', 'bin', 'col'), may hold values from -6 to 6
- focus_in: bfloat16 [64, 4096, 128], P('bin', 'row'), may hold values from -0.09375 to 0.09375
- focus_out: bfloat16 [64, 4096, 128], P('bin', 'row'), may hold values from -0.5 to 0.5
- start_basis: float32 [4096, 128], replicated, may hold values from -6 to 6
Outputs:
- covariance: float32 [4096, 4096], P('col', 'row')
- basis_out: float32 [4096, 128], P(('row', 'col'))
All inputs are finite; a program needn't handle non-finite values.
Results may differ from a plain program's by a relative error of at most 0.0045.
Values may be sent and summed in bfloat16 or wider, within the bound.
A program may use at most 128 MiB of HBM per device.

v0:
```python
import math
import jax
import jax.numpy as jnp
from jax import lax
from jax.sharding import PartitionSpec as P

ITERS = 2


def shards(snapshots, focus_in, focus_out, start_basis):
    rows_here, bins_here, snaps_here = snapshots.shape
    bin_count = lax.axis_size("bin")
    row_count = lax.axis_size("row")
    col_count = lax.axis_size("col")
    col_here = lax.axis_index("col")
    row_here = lax.axis_index("row")
    partial_proj = jnp.einsum(
        "mbs,bmr->brs", snapshots, focus_in, preferred_element_type=jnp.float32
    )
    projected = lax.psum(partial_proj, "row").astype(jnp.bfloat16)
    lifted = jnp.einsum("bmr,brs->mbs", focus_out, projected, preferred_element_type=jnp.float32)
    focused = (snapshots.astype(jnp.float32) + lifted).astype(jnp.bfloat16)
    columns = bins_here * snaps_here
    local_rows = focused.reshape(rows_here, columns)
    all_rows = lax.all_gather(local_rows, "row", axis=0, tiled=True)
    array_size = all_rows.shape[0]
    col_block = array_size // col_count
    piece_rows = col_block // bin_count
    scaling = 1.0 / (columns * col_count * bin_count)
    permuted = (
        all_rows.reshape(col_count, bin_count, piece_rows, columns)
        .transpose(1, 0, 2, 3)
        .reshape(array_size, columns)
    )
    share_rows = lax.psum_scatter(
        lax.dot_general(
            permuted, local_rows, (((1,), (1,)), ((), ())), preferred_element_type=jnp.float32
        ),
        ("bin", "col"),
        scatter_dimension=0,
        tiled=True,
    )
    tile_block = lax.all_gather(share_rows, "bin", axis=0, tiled=True)
    covariance = tile_block * scaling
    basis_now = start_basis
    for sweep_index in range(ITERS):
        col_rows = lax.dynamic_slice_in_dim(basis_now, col_here * col_block, col_block, 0)
        partial_image = lax.dot_general(
            covariance,
            col_rows,
            (((0,), (0,)), ((), ())),
            precision=lax.Precision.HIGHEST,
            preferred_element_type=jnp.float32,
        )
        row_sums = lax.psum(partial_image, "col")
        full_image = lax.all_gather(row_sums, "row", axis=0, tiled=True)
        gram_matrix = jnp.dot(
            full_image.T,
            full_image,
            precision=lax.Precision.HIGHEST,
            preferred_element_type=jnp.float32,
        )
        lower_factor = jnp.linalg.cholesky(gram_matrix)
        basis_now = jax.scipy.linalg.solve_triangular(lower_factor, full_image.T, lower=True).T
    out_rows = array_size // (row_count * col_count)
    mine_start = (row_here * col_count + col_here) * out_rows
    basis_out = lax.dynamic_slice_in_dim(basis_now, mine_start, out_rows, 0) * math.sqrt(array_size)
    return (covariance, basis_out)


def solution(mesh):
    in_specs = (P("row", "bin", "col"), P("bin", "row", None), P("bin", "row", None), P())
    out_specs = (P("col", "row"), P(("row", "col"), None))
    return jax.shard_map(shards, mesh=mesh, in_specs=in_specs, out_specs=out_specs, check_vma=False)
```

profile of v0, /device:TPU:1, one launch (start us, length us, event | category | flops | bytes accessed | tf_op | source)
XLA Modules:
  0.0 558.8 jit_solution(16705941478910044841)
XLA Ops:
  7.2 2.2 fusion.24
  9.4 14.6 %psum.21 = bf16[8,128,16]{1,2,0:T(8,128)(2,1)S(1)} all-reduce(f32[8,128,16]{1,2,0:T(8,128)S(1)} %fusion.24), channel_id=1, replica_groups=mesh['bin'=8,'row'=4,'col'=4] {'row'}, use_global_device_ids=true, to_apply=%region_0.0 | all-reduce | flops 16384 | bytes 98304 | tf_op jit(solution)/shard_map/psum | solution.py:20
  24.1 0.6 fusion.5
  24.7 0.9 copy.12
  25.6 27.7 %all-gather.5.cloned.1.call-done = bf16[4096,128]{1,0:T(8,128)(2,1)} async-done(((bf16[1024,128]{1,0:T(8,128)(2,1)}), bf16[4096,128]{1,0:T(8,128)(2,1)}) %all-gather.5.cloned.1.call-update) | async-done | bytes 1048592 | tf_op jit(solution)/shard_map/all_gather | solution.py:25
  53.3 1.3 copy.13
  54.7 8.0 %fusion.21 = f32[4096,1024]{1,0:T(8,128)} fusion(bf16[4096,128]{1,0:T(8,128)(2,1)S(1)} %bitcast.49, bf16[1024,128]{0,1:T(8,128)(2,1)S(1)} %bitcast.51), kind=kOutput, calls=%fused_computation.33 | convolution fusion | flops 1073741824 | bytes 18087936 | tf_op jit(solution)/shard_map/dot_general | solution.py:36
  62.8 184.6 %reduce-scatter.2.cloned.1.call-done = f32[128,1024]{1,0:T(8,128)} async-done(((f32[4096,1024]{1,0:T(8,128)}), f32[128,1024]{1,0:T(8,128)}) %reduce-scatter.2.cloned.1.call-update) | async-done | bytes 524304 | tf_op jit(solution)/shard_map/reduce_scatter | solution.py:35
  247.5 77.1 %all-gather.7.cloned.1.call-done = f32[1024,1024]{1,0:T(8,128)} async-done(((f32[128,1024]{1,0:T(8,128)}), f32[1024,1024]{1,0:T(8,128)}) %all-gather.7.cloned.1.call-update) | async-done | bytes 4194320 | tf_op jit(solution)/shard_map/all_gather | solution.py:43
  324.6 2.6 broadcast_multiply_fusion
  327.2 2.0 copy-done.1
  329.2 8.5 %fusion.8 = f32[1024,128]{1,0:T(8,128)} fusion(f32[1024,1024]{1,0:T(8,128)S(1)} %broadcast_multiply_fusion, f32[4096,128]{1,0:T(8,128)} %param.10, s32[]{:T(128)S(6)} %select_n.10), kind=kOutput, calls=%fused_computation.10 | convolution fusion | flops 1610612736 | bytes 5242884 | tf_op jit(solution)/shard_map/dot_general | solution.py:48
  337.8 36.4 %all-reduce.3.cloned.1.call-done = f32[1024,128]{1,0:T(8,128)} async-done(((f32[1024,128]{1,0:T(8,128)}), f32[1024,128]{1,0:T(8,128)}) %all-reduce.3.cloned.1.call-update) | async-done | bytes 524304 | tf_op jit(solution)/shard_map/psum | solution.py:55
  374.3 0.2 all-reduce.5.cloned.1.call-start
  374.5 32.6 %all-gather.9.cloned.1.call-done = f32[4096,128]{1,0:T(8,128)} async-done(((f32[1024,128]{1,0:T(8,128)}), f32[4096,128]{1,0:T(8,128)}) %all-gather.9.cloned.1.call-update) | async-done | bytes 2097168 | tf_op jit(solution)/shard_map/all_gather | solution.py:56
  407.1 5.7 %fusion.22 = f32[128,128]{1,0:T(8,128)S(1)} fusion(f32[4096,128]{1,0:T(8,128)} %all-gather.9.cloned.1.call-done), kind=kOutput, calls=%fused_computation.34 | convolution fusion | flops 805306368 | bytes 2162688 | tf_op jit(solution)/shard_map/dot_general | solution.py:57
  412.8 0.1 copy.14
  412.9 11.7 %cholesky.44 = f32[128,128]{1,0:T(8,128)S(1)} custom-call(f32[128,128]{1,0:T(8,128)S(1)} %fusion.15), custom_call_target="Cholesky" | custom-call | tf_op jit(solution)/shard_map/jit(cholesky)/cholesky | solution.py:63
  424.6 0.6 compare_reduce_fusion.1
  425.3 0.7 fusion.10
  425.9 9.8 %custom-call.6 = f32[1,128,128]{1,2,0:T(8,128)S(1)} custom-call(f32[1,128,128]{2,1,0:T(8,128)S(1)} %fusion.10), custom_call_target="InvertDiagBlocksLowerTriangular" | custom-call | tf_op jit(solution)/shard_map/jit(_solve_triangular)/triangular_solve | solution.py:64
  435.8 3.7 fusion.2
  439.4 7.8 %fusion.6 = f32[1024,128]{1,0:T(8,128)} fusion(f32[1024,1024]{1,0:T(8,128)S(1)} %copy-done.2, f32[128,4096]{1,0:T(8,128)S(1)} %fusion.2, s32[]{:T(128)S(6)} %select_n.10), kind=kOutput, calls=%fused_computation.8 | convolution fusion | flops 1610612736 | bytes 5242884 | tf_op jit(solution)/shard_map/dot_general | solution.py:48
  447.3 38.3 %all-reduce.5.cloned.1.call-done = f32[1024,128]{1,0:T(8,128)} async-done(((f32[1024,128]{1,0:T(8,128)}), f32[1024,128]{1,0:T(8,128)}) %all-reduce.5.cloned.1.call-update) | async-done | bytes 524304 | tf_op jit(solution)/shard_map/psum | solution.py:55
  485.6 33.0 %all-gather.11.cloned.1.call-done = f32[4096,128]{1,0:T(8,128)} async-done(((f32[1024,128]{1,0:T(8,128)}), f32[4096,128]{1,0:T(8,128)}) %all-gather.11.cloned.1.call-update) | async-done | bytes 2097168 | tf_op jit(solution)/shard_map/all_gather | solution.py:56
  518.6 5.7 %fusion.23 = f32[128,128]{1,0:T(8,128)S(1)} fusion(f32[4096,128]{1,0:T(8,128)} %all-gather.11.cloned.1.call-done), kind=kOutput, calls=%fused_computation.35 | convolution fusion | flops 805306368 | bytes 2162688 | tf_op jit(solution)/shard_map/dot_general | solution.py:57
  524.4 11.7 %cholesky.55 = f32[128,128]{1,0:T(8,128)S(1)} custom-call(f32[128,128]{1,0:T(8,128)S(1)} %fusion.13), custom_call_target="Cholesky" | custom-call | tf_op jit(solution)/shard_map/jit(cholesky)/cholesky | solution.py:63
  536.1 0.6 compare_reduce_fusion
  536.8 0.7 fusion.11
  537.4 9.8 %custom-call.7 = f32[1,128,128]{1,2,0:T(8,128)S(1)} custom-call(f32[1,128,128]{2,1,0:T(8,128)S(1)} %fusion.11), custom_call_target="InvertDiagBlocksLowerTriangular" | custom-call | tf_op jit(solution)/shard_map/jit(_solve_triangular)/triangular_solve | solution.py:64
  547.3 3.5 fusion
  550.8 0.8 copy.16
  (26 shorter events, 0.6 us)
Async XLA Ops:
  7.2 16.9 %copy-start = (bf16[8,1024,128]{2,1,0:T(8,128)(2,1)S(1)}, bf16[8,1024,128]{2,1,0:T(8,128)(2,1)}, u32[]{:S(2)}) copy-start(bf16[8,1024,128]{2,1,0:T(8,128)(2,1)} %param.9) | copy-start | bytes 6291460
  7.2 16.9 %copy-start.3 = (bf16[1024,8,16]{0,2,1:T(8,128)(2,1)S(1)}, bf16[1024,8,16]{0,2,1:T(8,128)(2,1)}, u32[]{:S(2)}) copy-start(bf16[1024,8,16]{0,2,1:T(8,128)(2,1)} %param.7) | copy-start | bytes 786436
  7.2 46.2 %all-gather.5.cloned.1.call-start = ((), (), s32[]{:S(2)}) async-start(), calls=%async_computation.1 | async-start | bytes 1310720 | tf_op jit(solution)/shard_map/all_gather | solution.py:25
  25.6 221.8 %reduce-scatter.2.cloned.1.call-start = ((), (), s32[]{:S(2)}) async-start(), calls=%async_computation.2 | async-start | bytes 17301504 | tf_op jit(solution)/shard_map/reduce_scatter | solution.py:35
  62.7 261.8 %all-gather.7.cloned.1.call-start = ((), (), s32[]{:S(2)}) async-start(), calls=%async_computation.3 | async-start | bytes 4718592 | tf_op jit(solution)/shard_map/all_gather | solution.py:43
  247.4 126.8 %all-reduce.3.cloned.1.call-start = ((), (), s32[]{:S(2)}) async-start(), calls=%async_computation.4 | async-start | bytes 1048576 | tf_op jit(solution)/shard_map/psum | solution.py:55
  327.2 2.0 copy-start.1
  337.8 69.3 %all-gather.9.cloned.1.call-start = ((), (), s32[]{:S(2)}) async-start(), calls=%async_computation.5 | async-start | bytes 2621440 | tf_op jit(solution)/shard_map/all_gather | solution.py:56
  374.3 111.3 %all-reduce.5.cloned.1.call-start = ((), (), s32[]{:S(2)}) async-start(), calls=%async_computation.6 | async-start | bytes 1048576 | tf_op jit(solution)/shard_map/psum | solution.py:55
  435.7 3.7 copy-start.2
  447.3 71.3 %all-gather.11.cloned.1.call-start = ((), (), s32[]{:S(2)}) async-start(), calls=%async_computation.7 | async-start | bytes 2621440 | tf_op jit(solution)/shard_map/all_gather | solution.py:56
Sparse Core Ops, SparseCore 0:
  25.7 27.5 all-gather.4
  62.9 184.4 reduce-scatter.1
  249.7 74.8 all-gather.6
  337.9 36.3 all-reduce.2
  375.8 31.2 all-gather.8
  447.4 38.1 all-reduce.4
  487.3 31.2 all-gather.10
where the time goes:
time: 567 us; the launch traced here: 559 us
  waiting for transfers between devices  430 us (76%)
  other arithmetic  48.4 us (9%)
  matrix products  45.7 us (8%)
  between operations  14.7 us (3%)
  blocking collectives  14.6 us (3%)
    reduce_scatter x1, waiting for transfers between devices, shards(): lax.psum_scatter(lax.dot_general(permuted, local_rows, (((1,), (1,)), (()...  185 us
    all_gather x1, waiting for transfers between devices, shards(): tile_block = lax.all_gather(share_rows, 'bin', axis=0, tiled=True)  77.1 us
    psum x2, waiting for transfers between devices, shards(): row_sums = lax.psum(partial_image, 'col')  74.7 us
    all_gather x2, waiting for transfers between devices, shards(): full_image = lax.all_gather(row_sums, 'row', axis=0, tiled=True)  65.5 us
    all_gather x1, waiting for transfers between devices, shards(): all_rows = lax.all_gather(local_rows, 'row', axis=0, tiled=True)  27.7 us
    another operation x6, other arithmetic, shards(): lower_factor = jnp.linalg.cholesky(gram_matrix)  24.8 us
    another operation x4, other arithmetic, shards(): jax.scipy.linalg.solve_triangular(lower_factor, full_image.T, lower=True)  20.9 us
    dot_general x2, matrix products, shards(): lax.dot_general(covariance, col_rows, (((0,), (0,)), ((), ())), precision...  16.3 us
  transfers between devices with their start and end apart: 7, of which 7 were waited for; matrix products, arithmetic and copies ran while one was open for 0% of the time, Pallas kernels for 0%

commit v1 on v0

--- a/solution.py
+++ b/solution.py
@@ -22,7 +22,8 @@
     focused = (snapshots.astype(jnp.float32) + lifted).astype(jnp.bfloat16)
     columns = bins_here * snaps_here
     local_rows = focused.reshape(rows_here, columns)
-    all_rows = lax.all_gather(local_rows, "row", axis=0, tiled=True)
+    copies = jnp.concatenate([local_rows] * lax.axis_size("row"), axis=0)
+    all_rows = lax.all_to_all(copies, "row", 0, 0, tiled=True)
     array_size = all_rows.shape[0]
     col_block = array_size // col_count
     piece_rows = col_block // bin_count

time: 567 us -> 557 us (0.982)
  waiting for transfers between devices: 430 us -> 406 us
  blocking collectives: 14.6 us -> 28.8 us
    all_gather x1 -> x0, waiting for transfers between devices: 27.7 us -> none  [shards(): all_rows = lax.all_gather(local_rows, 'row', axis=0, tiled=True)]
    all_to_all x0 -> x1, blocking collectives: none -> 14.2 us  [shards(): all_rows = lax.all_to_all(copies, 'row', 0, 0, tiled=True)]
  transfers between devices with their start and end apart: 7 -> 6, of which waited for: 7 -> 6; matrix products, arithmetic and copies ran while one was open for 0% -> 0% of each run, Pallas kernels for 0% -> 0%
where the time goes in v1:
time: 557 us; the launch traced here: 548 us
  waiting for transfers between devices  406 us (73%)
  other arithmetic  48.5 us (9%)
  matrix products  45.7 us (8%)
  blocking collectives  28.8 us (5%)
  between operations  14.7 us (3%)
    reduce_scatter x1, waiting for transfers between devices, shards(): lax.psum_scatter(lax.dot_general(permuted, local_rows, (((1,), (1,)), (()...  189 us
    all_gather x1, waiting for transfers between devices, shards(): tile_block = lax.all_gather(share_rows, 'bin', axis=0, tiled=True)  77.1 us
    psum x2, waiting for transfers between devices, shards(): row_sums = lax.psum(partial_image, 'col')  74.7 us
    all_gather x2, waiting for transfers between devices, shards(): full_image = lax.all_gather(row_sums, 'row', axis=0, tiled=True)  65.4 us
    another operation x6, other arithmetic, shards(): lower_factor = jnp.linalg.cholesky(gram_matrix)  24.8 us
    another operation x4, other arithmetic, shards(): jax.scipy.linalg.solve_triangular(lower_factor, full_image.T, lower=True)  20.9 us
    dot_general x2, matrix products, shards(): lax.dot_general(covariance, col_rows, (((0,), (0,)), ((), ())), precision...  16.3 us
    psum x1, blocking collectives, shards(): projected = lax.psum(partial_proj, 'row').astype(jnp.bfloat16)  14.6 us
  transfers between devices with their start and end apart: 6, of which 6 were waited for; matrix products, arithmetic and copies ran while one was open for 0% of the time, Pallas kernels for 0%

profile of v1, /device:TPU:1, one launch (start us, length us, event | category | flops | bytes accessed | tf_op | source)
XLA Modules:
  0.0 548.4 jit_solution(7723025520213440278)
XLA Ops:
  7.2 2.2 fusion.24
  9.4 14.6 %psum.21 = bf16[8,128,16]{1,2,0:T(8,128)(2,1)S(1)} all-reduce(f32[8,128,16]{1,2,0:T(8,128)S(1)} %fusion.24), channel_id=1, replica_groups=mesh['bin'=8,'row'=4,'col'=4] {'row'}, use_global_device_ids=true, to_apply=%region_0.0 | all-reduce | flops 16384 | bytes 98304 | tf_op jit(solution)/shard_map/psum | solution.py:20
  24.1 0.6 fusion.5
  24.7 0.1 pad_maximum_fusion
  24.9 1.3 copy.12
  26.2 14.2 %all_to_all.9 = bf16[4,1024,128]{2,1,0:T(8,128)(2,1)S(1)} all-to-all(bf16[4,1024,128]{2,1,0:T(8,128)(2,1)} %bitcast.51), channel_id=1, replica_groups=mesh['bin'=8,'row'=4,'col'=4] {'row'}, dimensions={0} | all-to-all | bytes 2097152 | tf_op jit(solution)/shard_map/all_to_all | solution.py:26
  40.4 8.0 %fusion.21 = f32[4096,1024]{1,0:T(8,128)} fusion(bf16[4096,128]{1,0:T(8,128)(2,1)S(1)} %bitcast.50, bf16[1024,128]{0,1:T(8,128)(2,1)S(1)} %bitcast.54), kind=kOutput, calls=%fused_computation.34 | convolution fusion | flops 1073741824 | bytes 18087936 | tf_op jit(solution)/shard_map/dot_general | solution.py:37
  48.5 188.5 %reduce-scatter.2.cloned.1.call-done = f32[128,1024]{1,0:T(8,128)} async-done(((f32[4096,1024]{1,0:T(8,128)}), f32[128,1024]{1,0:T(8,128)}) %reduce-scatter.2.cloned.1.call-update) | async-done | bytes 524304 | tf_op jit(solution)/shard_map/reduce_scatter | solution.py:36
  237.2 77.1 %all-gather.4.cloned.1.call-done = f32[1024,1024]{1,0:T(8,128)} async-done(((f32[128,1024]{1,0:T(8,128)}), f32[1024,1024]{1,0:T(8,128)}) %all-gather.4.cloned.1.call-update) | async-done | bytes 4194320 | tf_op jit(solution)/shard_map/all_gather | solution.py:44
  314.3 2.6 broadcast_multiply_fusion
  316.9 2.0 copy-done.1
  318.9 8.5 %fusion.8 = f32[1024,128]{1,0:T(8,128)} fusion(f32[1024,1024]{1,0:T(8,128)S(1)} %broadcast_multiply_fusion, f32[4096,128]{1,0:T(8,128)} %param.10, s32[]{:T(128)S(6)} %select_n.10), kind=kOutput, calls=%fused_computation.11 | convolution fusion | flops 1610612736 | bytes 5242884 | tf_op jit(solution)/shard_map/dot_general | solution.py:49
  327.5 36.4 %all-reduce.3.cloned.1.call-done = f32[1024,128]{1,0:T(8,128)} async-done(((f32[1024,128]{1,0:T(8,128)}), f32[1024,128]{1,0:T(8,128)}) %all-reduce.3.cloned.1.call-update) | async-done | bytes 524304 | tf_op jit(solution)/shard_map/psum | solution.py:56
  364.0 0.2 all-reduce.5.cloned.1.call-start
  364.2 32.6 %all-gather.6.cloned.1.call-done = f32[4096,128]{1,0:T(8,128)} async-done(((f32[1024,128]{1,0:T(8,128)}), f32[4096,128]{1,0:T(8,128)}) %all-gather.6.cloned.1.call-update) | async-done | bytes 2097168 | tf_op jit(solution)/shard_map/all_gather | solution.py:57
  396.8 5.7 %fusion.22 = f32[128,128]{1,0:T(8,128)S(1)} fusion(f32[4096,128]{1,0:T(8,128)} %all-gather.6.cloned.1.call-done), kind=kOutput, calls=%fused_computation.35 | convolution fusion | flops 805306368 | bytes 2162688 | tf_op jit(solution)/shard_map/dot_general | solution.py:58
  402.5 0.1 copy.14
  402.6 11.7 %cholesky.44 = f32[128,128]{1,0:T(8,128)S(1)} custom-call(f32[128,128]{1,0:T(8,128)S(1)} %fusion.15), custom_call_target="Cholesky" | custom-call | tf_op jit(solution)/shard_map/jit(cholesky)/cholesky | solution.py:64
  414.3 0.6 compare_reduce_fusion.1
  415.0 0.7 fusion.10
  415.6 9.8 %custom-call.6 = f32[1,128,128]{1,2,0:T(8,128)S(1)} custom-call(f32[1,128,128]{2,1,0:T(8,128)S(1)} %fusion.10), custom_call_target="InvertDiagBlocksLowerTriangular" | custom-call | tf_op jit(solution)/shard_map/jit(_solve_triangular)/triangular_solve | solution.py:65
  425.5 3.7 fusion.2
  429.2 7.8 %fusion.6 = f32[1024,128]{1,0:T(8,128)} fusion(f32[1024,1024]{1,0:T(8,128)S(1)} %copy-done.2, f32[128,4096]{1,0:T(8,128)S(1)} %fusion.2, s32[]{:T(128)S(6)} %select_n.10), kind=kOutput, calls=%fused_computation.9 | convolution fusion | flops 1610612736 | bytes 5242884 | tf_op jit(solution)/shard_map/dot_general | solution.py:49
  437.0 38.3 %all-reduce.5.cloned.1.call-done = f32[1024,128]{1,0:T(8,128)} async-done(((f32[1024,128]{1,0:T(8,128)}), f32[1024,128]{1,0:T(8,128)}) %all-reduce.5.cloned.1.call-update) | async-done | bytes 524304 | tf_op jit(solution)/shard_map/psum | solution.py:56
  475.4 32.8 %all-gather.8.cloned.1.call-done = f32[4096,128]{1,0:T(8,128)} async-done(((f32[1024,128]{1,0:T(8,128)}), f32[4096,128]{1,0:T(8,128)}) %all-gather.8.cloned.1.call-update) | async-done | bytes 2097168 | tf_op jit(solution)/shard_map/all_gather | solution.py:57
  508.2 5.7 %fusion.23 = f32[128,128]{1,0:T(8,128)S(1)} fusion(f32[4096,128]{1,0:T(8,128)} %all-gather.8.cloned.1.call-done), kind=kOutput, calls=%fused_computation.36 | convolution fusion | flops 805306368 | bytes 2162688 | tf_op jit(solution)/shard_map/dot_general | solution.py:58
  514.0 11.7 %cholesky.55 = f32[128,128]{1,0:T(8,128)S(1)} custom-call(f32[128,128]{1,0:T(8,128)S(1)} %fusion.13), custom_call_target="Cholesky" | custom-call | tf_op jit(solution)/shard_map/jit(cholesky)/cholesky | solution.py:64
  525.7 0.6 compare_reduce_fusion
  526.4 0.7 fusion.11
  527.0 9.8 %custom-call.7 = f32[1,128,128]{1,2,0:T(8,128)S(1)} custom-call(f32[1,128,128]{2,1,0:T(8,128)S(1)} %fusion.11), custom_call_target="InvertDiagBlocksLowerTriangular" | custom-call | tf_op jit(solution)/shard_map/jit(_solve_triangular)/triangular_solve | solution.py:65
  536.8 3.5 fusion
  540.4 0.8 copy.16
  (25 shorter events, 0.6 us)
Async XLA Ops:
  7.2 16.9 %copy-start = (bf16[8,1024,128]{2,1,0:T(8,128)(2,1)S(1)}, bf16[8,1024,128]{2,1,0:T(8,128)(2,1)}, u32[]{:S(2)}) copy-start(bf16[8,1024,128]{2,1,0:T(8,128)(2,1)} %param.9) | copy-start | bytes 6291460
  7.2 16.9 %copy-start.3 = (bf16[1024,8,16]{0,2,1:T(8,128)(2,1)S(1)}, bf16[1024,8,16]{0,2,1:T(8,128)(2,1)}, u32[]{:S(2)}) copy-start(bf16[1024,8,16]{0,2,1:T(8,128)(2,1)} %param.7) | copy-start | bytes 786436
  7.2 229.9 %reduce-scatter.2.cloned.1.call-start = ((), (), s32[]{:S(2)}) async-start(), calls=%async_computation.2 | async-start | bytes 17301504 | tf_op jit(solution)/shard_map/reduce_scatter | solution.py:36
  48.5 265.8 %all-gather.4.cloned.1.call-start = ((), (), s32[]{:S(2)}) async-start(), calls=%async_computation.3 | async-start | bytes 4718592 | tf_op jit(solution)/shard_map/all_gather | solution.py:44
  237.1 126.9 %all-reduce.3.cloned.1.call-start = ((), (), s32[]{:S(2)}) async-start(), calls=%async_computation.4 | async-start | bytes 1048576 | tf_op jit(solution)/shard_map/psum | solution.py:56
  316.9 2.0 copy-start.1
  327.5 69.3 %all-gather.6.cloned.1.call-start = ((), (), s32[]{:S(2)}) async-start(), calls=%async_computation.5 | async-start | bytes 2621440 | tf_op jit(solution)/shard_map/all_gather | solution.py:57
  364.0 111.4 %all-reduce.5.cloned.1.call-start = ((), (), s32[]{:S(2)}) async-start(), calls=%async_computation.6 | async-start | bytes 1048576 | tf_op jit(solution)/shard_map/psum | solution.py:56
  425.5 3.7 copy-start.2
  437.0 71.2 %all-gather.8.cloned.1.call-start = ((), (), s32[]{:S(2)}) async-start(), calls=%async_computation.7 | async-start | bytes 2621440 | tf_op jit(solution)/shard_map/all_gather | solution.py:57
Sparse Core Ops, SparseCore 0:
  48.6 188.4 reduce-scatter.1
  239.4 74.8 all-gather.3
  327.6 36.3 all-reduce.2
  365.5 31.2 all-gather.5
  437.1 38.1 all-reduce.4
  476.9 31.2 all-gather.7
